TPU v7x, 32 devices: a whole 2x2x4 slice. The times are simulated.
32 devices in a mesh: chan: 4 (over y, core), tile: 8 (over z, x).
Axes of the slice: x: 2, y: 2, z: 4, core: 2. Of those that a mesh axis runs over, the one named last changes fastest.
Arguments:
- intensity: bfloat16 [256, 256, 512], P('chan', 'tile'), may hold values from -12 to 12
- block_pick: int32 [8, 4, 4], P('tile', 'chan'), may hold values from 0 to 7, as said below
- owner_tile: int32 [8, 4, 4], P('tile', 'chan'), may hold values from 0 to 7, as said below
- source_index: int32 [8, 4, 4], P('tile', 'chan'), may hold values from 0 to 15
- mask_low: int32 [8, 4, 4, 1024], P('tile', 'chan'), may hold values from 0 to 63
- mask_high: int32 [8, 4, 4, 1024], P('tile', 'chan'), may hold values from 64 to 128
Outputs:
- moment_maps: float32 [8, 4, 8, 2, 1024], P('tile', 'chan')
- spectra: float32 [8, 4, 16, 256], P('tile', 'chan')
- smoothed: bfloat16 [256, 256, 512], P(None, 'tile', 'chan')
Inputs may be any that keep to these rules, and one draw needn't show every extreme that they name: `block_pick`: the 4 block numbers of one device are distinct. `owner_tile`: among the 4 sends of one device no owner appears more than 2 times; in every chan index some owner receives exactly 2 blocks from every device of that chan index.
All inputs are finite; a program needn't handle non-finite values.
Results may differ from a plain program's by a relative error of at most 0.0021.
Values may be sent and summed in bfloat16 or wider, within the bound.
A program may use at most 128 MiB of HBM per device.

v0:
```python
import jax
import jax.numpy as jnp
from jax import lax
from jax.sharding import PartitionSpec as P

BCH = 128
BPIX = 32
RADIUS = 2
CAP = 2
SRC_DEV = 16
SIGMA = 1.5


def with_halo(block, sides, width):
    for axis, dim in sides:
        count = lax.axis_size(axis)
        forward = [(i, i + 1) for i in range(count - 1)]
        backward = [(target, source) for source, target in forward]
        low = lax.ppermute(
            lax.slice_in_dim(block, block.shape[dim] - width, None, axis=dim), axis, forward
        )
        high = lax.ppermute(lax.slice_in_dim(block, 0, width, axis=dim), axis, backward)
        block = jnp.concatenate([low, block, high], axis=dim)
    return block


def gauss_weights():
    offsets = jnp.arange(-RADIUS, RADIUS + 1).astype(jnp.float32)
    raw_weights = jnp.exp(-offsets * offsets / (2.0 * SIGMA * SIGMA))
    return raw_weights / jnp.sum(raw_weights)


def smooth_tiles(framed):
    chan_total = framed.shape[0]
    rows_inner = framed.shape[1] - 2 * RADIUS
    cols_inner = framed.shape[2] - 2 * RADIUS
    chan_blocks = chan_total // BCH
    weights = gauss_weights()

    def smooth_block(block_index):
        first_chan = block_index * BCH
        middle = lax.dynamic_slice_in_dim(framed, first_chan, BCH, 0).astype(jnp.float32)
        before = lax.dynamic_slice_in_dim(framed, jnp.maximum(first_chan - 1, 0), 1, 0).astype(
            jnp.float32
        )
        before = before * (block_index > 0).astype(jnp.float32)
        after = lax.dynamic_slice_in_dim(
            framed, jnp.minimum(first_chan + BCH, chan_total - 1), 1, 0
        ).astype(jnp.float32)
        after = after * (block_index < chan_blocks - 1).astype(jnp.float32)
        lower = jnp.concatenate([before, middle[:-1]], axis=0)
        upper = jnp.concatenate([middle[1:], after], axis=0)
        hanning = 0.5 * middle + 0.25 * (lower + upper)
        row_pass = sum(
            (
                weights[offset] * hanning[:, offset : offset + rows_inner, :]
                for offset in range(2 * RADIUS + 1)
            )
        )
        col_pass = sum(
            (
                weights[offset] * row_pass[:, :, offset : offset + cols_inner]
                for offset in range(2 * RADIUS + 1)
            )
        )
        return col_pass.astype(jnp.bfloat16)

    stacked = lax.map(smooth_block, jnp.arange(chan_blocks, dtype=jnp.int32))
    return stacked.reshape(chan_total, rows_inner, cols_inner)


def per_device(intensity, block_pick, owner_tile, source_index, mask_low, mask_high):
    regrouped = lax.all_to_all(intensity, "chan", split_axis=2, concat_axis=0, tiled=True)
    framed = with_halo(regrouped, (("chan", 2), ("tile", 1)), RADIUS)
    tile_cube = smooth_tiles(framed)
    chan_total, rows_inner, cols_inner = tile_cube.shape
    chan_blocks = chan_total // BCH
    block_rows = rows_inner // BPIX
    block_cols = cols_inner // BPIX
    per_chan_block = block_rows * block_cols
    pixel_count = mask_low.shape[-1]
    picks = block_pick.reshape(-1)
    owners = owner_tile.reshape(-1)
    sources = source_index.reshape(-1)
    send_count = picks.shape[0]
    low_rows = mask_low.reshape(send_count, pixel_count)
    high_rows = mask_high.reshape(send_count, pixel_count)
    chan_of = picks // per_chan_block
    positions = jnp.arange(send_count, dtype=jnp.int32)
    earlier = (positions[None, :] < positions[:, None]) & (owners[None, :] == owners[:, None])
    ranking = jnp.sum(earlier.astype(jnp.int32), axis=1)
    slot_of = owners * CAP + ranking
    peer_count = lax.axis_size("tile")
    slot_total = peer_count * CAP
    filled = slot_of[None, :] == jnp.arange(slot_total, dtype=jnp.int32)[:, None]
    occupied = jnp.any(filled, axis=1)
    sender = jnp.sum(jnp.where(filled, positions[None, :], 0), axis=1)
    tags = jnp.stack([jnp.where(occupied, sources[sender], -1), chan_of[sender]], axis=1).reshape(
        peer_count, CAP, 2
    )
    block_total = chan_blocks * per_chan_block
    low_grid = jnp.zeros((block_total, pixel_count), jnp.int32).at[picks].set(low_rows)
    high_grid = jnp.zeros((block_total, pixel_count), jnp.int32).at[picks].set(high_rows)

    def to_tile(grid):
        shaped = grid.reshape(chan_blocks, block_rows, block_cols, BPIX, BPIX).transpose(
            0, 1, 3, 2, 4
        )
        return shaped.reshape(chan_blocks, 1, rows_inner, cols_inner)

    low_tile = to_tile(low_grid)
    high_tile = to_tile(high_grid)
    cube_blocks = tile_cube.reshape(chan_blocks, BCH, rows_inner, cols_inner)
    chan_pos = jnp.arange(BCH, dtype=jnp.int32).reshape(1, BCH, 1, 1)
    inside = (low_tile <= chan_pos) & (chan_pos < high_tile)
    masked = jnp.where(inside, cube_blocks.astype(jnp.float32), 0.0)
    maps_tile = jnp.sum(masked, axis=1)
    spectra_tile = jnp.sum(
        masked.reshape(chan_blocks, BCH, block_rows, BPIX, block_cols, BPIX), axis=(3, 5)
    )
    all_maps = (
        maps_tile.reshape(chan_blocks, block_rows, BPIX, block_cols, BPIX)
        .transpose(0, 1, 3, 2, 4)
        .reshape(block_total, pixel_count)
    )
    all_spectra = spectra_tile.transpose(0, 2, 3, 1).reshape(block_total, BCH)
    slot_picks = picks[sender]
    maps_slots = jnp.where(occupied[:, None], all_maps[slot_picks], 0.0).reshape(
        peer_count, CAP, pixel_count
    )
    spectra_slots = jnp.where(occupied[:, None], all_spectra[slot_picks], 0.0).reshape(
        peer_count, CAP, BCH
    )
    maps_here, spectra_here, tags_here = (
        lax.all_to_all(maps_slots, "tile", split_axis=0, concat_axis=0, tiled=True),
        lax.all_to_all(spectra_slots, "tile", split_axis=0, concat_axis=0, tiled=True),
        lax.all_to_all(tags, "tile", split_axis=0, concat_axis=0, tiled=True),
    )
    moment_maps = maps_here.reshape(1, 1, peer_count, CAP, pixel_count)
    keys_here = (tags_here[..., 0] * chan_blocks + tags_here[..., 1]).reshape(-1)
    selector = (
        keys_here[None, :] == jnp.arange(SRC_DEV * chan_blocks, dtype=jnp.int32)[:, None]
    ).astype(jnp.float32)
    spectra = jnp.dot(
        selector,
        spectra_here.reshape(-1, BCH),
        precision=lax.Precision.HIGHEST,
        preferred_element_type=jnp.float32,
    )
    return (moment_maps, spectra.reshape(1, 1, SRC_DEV, chan_blocks * BCH), tile_cube)


def solution(mesh):
    return jax.shard_map(
        per_device,
        mesh=mesh,
        in_specs=(
            P("chan", "tile", None),
            P("tile", "chan", None),
            P("tile", "chan", None),
            P("tile", "chan", None),
            P("tile", "chan", None, None),
            P("tile", "chan", None, None),
        ),
        out_specs=(
            P("tile", "chan", None, None, None),
            P("tile", "chan", None, None),
            P(None, "tile", "chan"),
        ),
        check_vma=False,
    )
```

profile of v0, /device:TPU:4, one launch (start us, length us, event | category | flops | bytes accessed | tf_op | source)
XLA Modules:
  0.0 183.7 jit_solution(6895373197032733767)
XLA Ops:
  0.6 8.8 %copy.87 = bf16[64,32,512]{0,1,2:T(8,128)(2,1)} copy(bf16[64,32,512]{2,1,0:T(8,128)(2,1)} %param.8) | data formatting | bytes 4194304 | tf_op args[0]
  9.4 5.9 %reshape.268 = bf16[4,2,131072]{2,1,0:T(2,128)(2,1)} reshape(bf16[512,32,64]{2,1,0:T(8,128)(2,1)} %bitcast.84) | data formatting | bytes 4194304
  15.3 3.7 %all-to-all-start = ((bf16[4,2,131072]{2,1,0:T(2,128)(2,1)}), bf16[4,2,131072]{2,1,0:T(2,128)(2,1)S(1)}, u32[]{:S(2)}, u32[]{:S(2)}) async-start(bf16[4,2,131072]{2,1,0:T(2,128)(2,1)} %reshape.268), calls=%async_computation | async-start | bytes 4194304 | tf_op jit(solution)/shard_map/all_to_all | solution.py:73
  22.3 20.5 %all-to-all-done = bf16[4,2,131072]{2,1,0:T(2,128)(2,1)S(1)} async-done(((bf16[4,2,131072]{2,1,0:T(2,128)(2,1)}), bf16[4,2,131072]{2,1,0:T(2,128)(2,1)S(1)}, u32[]{:S(2)}, u32[]{:S(2)}) %all-to-all-start) | async-done | bytes 2097184 | tf_op jit(solution)/shard_map/all_to_all | solution.py:73
  42.8 6.6 %all-to-all-start.2 = ((s32[8,2,2]{1,2,0:T(2,128)}), s32[8,2,2]{1,2,0:T(2,128)S(1)}, u32[]{:S(2)}, u32[]{:S(2)}) async-start(s32[8,2,2]{1,2,0:T(2,128)} %copy.98), calls=%async_computation.2 | async-start | bytes 16384 | tf_op jit(solution)/shard_map/all_to_all | solution.py:137
  49.4 4.0 %reshape.269 = bf16[512,32,64]{2,1,0:T(8,128)(2,1)} reshape(bf16[4,2,131072]{2,1,0:T(2,128)(2,1)S(1)} %all-to-all-done) | data formatting | bytes 4194304
  53.4 6.8 %copy.102 = bf16[64,32,4,128]{3,2,1,0:T(4,128)(2,1)} copy(bf16[64,32,4,128]{0,1,3,2:T(8,128)(2,1)} %bitcast.83) | data formatting | bytes 4194304 | tf_op jit(solution)/shard_map/all_to_all | solution.py:73
  70.3 3.3 %copy.91 = bf16[256,32,2]{0,1,2:T(8,128)(2,1)S(1)} copy(bf16[256,32,2]{2,1,0:T(8,128)(2,1)} %get-tuple-element.93) | data formatting | bytes 65536 | tf_op jit(solution)/shard_map/slice | solution.py:22
  73.6 3.8 %collective-permute-start.1 = (bf16[256,32,2]{0,1,2:T(8,128)(2,1)S(1)}, bf16[256,32,2]{0,1,2:T(8,128)(2,1)S(1)}, u32[]{:S(2)}, u32[]{:S(2)}) collective-permute-start(bf16[256,32,2]{0,1,2:T(8,128)(2,1)S(1)} %copy.91), channel_id=1, source_target_pairs={{8,0},{16,8},{24,16},{9,1},{17,9},{25,17},{10,2},{18,10},{26,18},{... | collective-permute-start | bytes 98312 | tf_op jit(solution)/shard_map/ppermute | solution.py:22
  78.0 4.2 %copy.92 = bf16[256,32,2]{2,1,0:T(8,128)(2,1)} copy(bf16[256,32,2]{0,1,2:T(8,128)(2,1)S(1)} %collective-permute-done) | data formatting | bytes 65536 | tf_op jit(solution)/shard_map/ppermute | solution.py:19
  82.3 4.2 %copy.93 = bf16[256,32,2]{2,1,0:T(8,128)(2,1)} copy(bf16[256,32,2]{0,1,2:T(8,128)(2,1)S(1)} %collective-permute-done.1) | data formatting | bytes 65536 | tf_op jit(solution)/shard_map/ppermute | solution.py:22
  86.5 4.3 %pad_maximum_fusion = bf16[256,32,132]{2,1,0:T(8,128)(2,1)S(1)} fusion(bf16[256,32,2]{2,1,0:T(8,128)(2,1)} %copy.93, bf16[256,32,128]{2,1,0:T(8,128)(2,1)S(1)} %bitcast.82, bf16[256,32,2]{2,1,0:T(8,128)(2,1)} %copy.92), kind=kLoop, calls=%fused_computation.33 | loop fusion | flops 6488064 | bytes 4325376 | tf_op jit(solution)/shard_map/concatenate | solution.py:23
  93.1 3.9 %collective-permute-start.2 = (bf16[256,2,132]{2,1,0:T(2,128)(2,1)S(1)}, bf16[256,2,132]{2,1,0:T(2,128)(2,1)S(1)}, u32[]{:S(2)}, u32[]{:S(2)}) collective-permute-start(bf16[256,2,132]{2,1,0:T(2,128)(2,1)S(1)} %get-tuple-element.90), channel_id=1, source_target_pairs={{0,1},{1,2},{2,3},{3,4},{4,5},{5,6},{6,7},{8,9},{9,10},{10,11},{11... | collective-permute-start | bytes 405512 | tf_op jit(solution)/shard_map/ppermute | solution.py:19
  101.3 7.6 %copy.95 = bf16[256,32,132]{0,2,1:T(8,128)(2,1)} copy(bf16[256,32,132]{2,1,0:T(8,128)(2,1)} %copy-done.5) | data formatting | bytes 4325376 | tf_op jit(solution)/shard_map/concatenate | solution.py:23
  111.2 38.9 %while.12 = (s32[]{:T(128)}, bf16[2,128,32,128]{1,3,2,0:T(8,128)(2,1)}, f32[5]{0:T(128)S(1)}, s32[2]{0:T(128)S(1)}, bf16[256,36,132]{0,2,1:T(8,128)(2,1)S(1)}, /...) while((s32[]{:T(128)}, ...), condition=%wide.region_6.7_spmd, body=%wide.region_5.6_spmd.sunk | while | flops 14994001 | bytes 46544248 | solution.py:68
  121.4 3.8 %fusion.43 = f32[128,32,132]{0,2,1:T(8,128)S(1)} fusion(f32[128,36,132]{0,2,1:T(8,128)S(1)} %fusion.41, f32[]{:T(128)} %bitcast.74, f32[]{:T(128)} %bitcast.75, f32[]{:T(128)} %bitcast.76, f32[]{:T(128)} %bitcast.77, f32[]{:T(128)} %bitcast.78), kind=kLoop, calls=%fused_computation.13.clone.1 | loop fusion | flops 4866048 | bytes 12976148 | tf_op jit(solution)/shard_map/while/body/eval_jaxpr/add | solution.py:54
  125.3 5.4 %bitcast_dynamic-update-slice_fusion.2 = bf16[2,128,32,128]{1,3,2,0:T(8,128)(2,1)} fusion(bf16[2,128,32,128]{1,3,2,0:T(8,128)(2,1)} %get-tuple-element.158, s32[]{:T(128)} %get-tuple-element.157, f32[128,32,132]{0,2,1:T(8,128)S(1)} %fusion.43, f32[]{:T(128)} %bitcast.74, f32[]{:T(128)} %bitcast.75, f32[]{:T(128)} %bitcast.76, f32[]{:T(128)} %bitcast.77, ...), kind=kLoop, calls=%fused_computation.32.clone.1 | loop fusion | flops 5242880 | bytes 11537408 | tf_op jit(solution)/shard_map/while/body/jit(dynamic_update_index_in_dim)/dynamic_update_slice | solution.py:68
  140.9 3.8 %fusion.43 = f32[128,32,132]{0,2,1:T(8,128)S(1)} fusion(f32[128,36,132]{0,2,1:T(8,128)S(1)} %fusion.41, f32[]{:T(128)} %bitcast.74, f32[]{:T(128)} %bitcast.75, f32[]{:T(128)} %bitcast.76, f32[]{:T(128)} %bitcast.77, f32[]{:T(128)} %bitcast.78), kind=kLoop, calls=%fused_computation.13.clone.1 | loop fusion | flops 4866048 | bytes 12976148 | tf_op jit(solution)/shard_map/while/body/eval_jaxpr/add | solution.py:54
  144.7 5.4 %bitcast_dynamic-update-slice_fusion.2 = bf16[2,128,32,128]{1,3,2,0:T(8,128)(2,1)} fusion(bf16[2,128,32,128]{1,3,2,0:T(8,128)(2,1)} %get-tuple-element.158, s32[]{:T(128)} %get-tuple-element.157, f32[128,32,132]{0,2,1:T(8,128)S(1)} %fusion.43, f32[]{:T(128)} %bitcast.74, f32[]{:T(128)} %bitcast.75, f32[]{:T(128)} %bitcast.76, f32[]{:T(128)} %bitcast.77, ...), kind=kLoop, calls=%fused_computation.32.clone.1 | loop fusion | flops 5242880 | bytes 11537408 | tf_op jit(solution)/shard_map/while/body/jit(dynamic_update_index_in_dim)/dynamic_update_slice | solution.py:68
  150.1 6.1 %fusion.11 = (f32[2,128,128]{1,2,0:T(8,128)S(1)}, f32[2,32,128]{2,1,0:T(8,128)S(1)}) fusion(bf16[2,128,32,128]{1,3,2,0:T(8,128)(2,1)} %get-tuple-element.68, s32[2,32,128]{2,1,0:T(8,128)S(1)} %lt.89, s32[2,32,128]{2,1,0:T(8,128)S(1)} %le.17), kind=kLoop, calls=%fused_computation.35 | loop fusion | flops 7299072 | bytes 2326528 | tf_op jit(solution)/shard_map/reduce_sum | solution.py:118
  157.5 6.6 %all-to-all-start.3 = ((f32[8,2,128]{2,1,0:T(2,128)}), f32[8,2,128]{2,1,0:T(2,128)S(1)}, u32[]{:S(2)}, u32[]{:S(2)}) async-start(f32[8,2,128]{2,1,0:T(2,128)} %broadcast_select_fusion.1), calls=%async_computation.3 | async-start | bytes 16384 | tf_op jit(solution)/shard_map/all_to_all | solution.py:136
  165.7 4.5 %copy.101 = bf16[2,128,32,128]{3,2,1,0:T(8,128)(2,1)} copy(bf16[2,128,32,128]{1,3,2,0:T(8,128)(2,1)} %get-tuple-element.68) | data formatting | bytes 4194304 | tf_op jit(solution)/shard_map/while | solution.py:68
  170.6 5.6 %all-to-all-start.1 = ((f32[8,2,1024]{2,1,0:T(2,128)}), f32[8,2,1024]{2,1,0:T(2,128)S(1)}, u32[]{:S(2)}, u32[]{:S(2)}) async-start(f32[8,2,1024]{2,1,0:T(2,128)} %broadcast_select_fusion), calls=%async_computation.1 | async-start | bytes 131072 | tf_op jit(solution)/shard_map/all_to_all | solution.py:135
  176.9 6.2 %all-to-all-done.1 = f32[8,2,1024]{2,1,0:T(2,128)S(1)} async-done(((f32[8,2,1024]{2,1,0:T(2,128)}), f32[8,2,1024]{2,1,0:T(2,128)S(1)}, u32[]{:S(2)}, u32[]{:S(2)}) %all-to-all-start.1) | async-done | bytes 65568 | tf_op jit(solution)/shard_map/all_to_all | solution.py:135
  (92 shorter events, 43.8 us)
Async XLA Ops:
  0.6 98.4 %copy-start = (s32[1,1,4,1024]{3,2,1,0:T(4,128)S(1)}, s32[1,1,4,1024]{3,2,1,0:T(4,128)}, u32[]{:S(2)}) copy-start(s32[1,1,4,1024]{3,2,1,0:T(4,128)} %param.12) | copy-start | bytes 49156
  15.3 3.8 %copy-start.7 = (s32[1,1,4]{2,1,0:T(1,128)S(1)}, s32[1,1,4]{2,1,0:T(1,128)}, u32[]{:S(2)}) copy-start(s32[1,1,4]{2,1,0:T(1,128)} %param.10) | copy-start | bytes 52
  15.3 4.1 %copy-start.2 = (s32[1,1,4]{2,1,0:T(1,128)S(1)}, s32[1,1,4]{2,1,0:T(1,128)}, u32[]{:S(2)}) copy-start(s32[1,1,4]{2,1,0:T(1,128)} %param.9) | copy-start | bytes 52
  15.3 4.7 %copy-start.1 = (s32[1,1,4]{2,1,0:T(1,128)S(1)}, s32[1,1,4]{2,1,0:T(1,128)}, u32[]{:S(2)}) copy-start(s32[1,1,4]{2,1,0:T(1,128)} %param.11) | copy-start | bytes 52
  15.3 27.5 %all-to-all-start = ((bf16[4,2,131072]{2,1,0:T(2,128)(2,1)}), bf16[4,2,131072]{2,1,0:T(2,128)(2,1)S(1)}, u32[]{:S(2)}, u32[]{:S(2)}) async-start(bf16[4,2,131072]{2,1,0:T(2,128)(2,1)} %reshape.268), calls=%async_computation | async-start | bytes 4194304 | tf_op jit(solution)/shard_map/all_to_all | solution.py:73
  42.8 58.4 %all-to-all-start.2 = ((s32[8,2,2]{1,2,0:T(2,128)}), s32[8,2,2]{1,2,0:T(2,128)S(1)}, u32[]{:S(2)}, u32[]{:S(2)}) async-start(s32[8,2,2]{1,2,0:T(2,128)} %copy.98), calls=%async_computation.2 | async-start | bytes 16384 | tf_op jit(solution)/shard_map/all_to_all | solution.py:137
  68.4 9.7 %collective-permute-start = (bf16[256,32,2]{0,1,2:T(8,128)(2,1)S(1)}, bf16[256,32,2]{0,1,2:T(8,128)(2,1)S(1)}, u32[]{:S(2)}, u32[]{:S(2)}) collective-permute-start(bf16[256,32,2]{0,1,2:T(8,128)(2,1)S(1)} %copy.90), channel_id=1, source_target_pairs={{0,8},{8,16},{16,24},{1,9},{9,17},{17,25},{2,10},{10,18},{18,26},{... | collective-permute-start | bytes 98312 | tf_op jit(solution)/shard_map/ppermute | solution.py:19
  73.6 8.7 %collective-permute-start.1 = (bf16[256,32,2]{0,1,2:T(8,128)(2,1)S(1)}, bf16[256,32,2]{0,1,2:T(8,128)(2,1)S(1)}, u32[]{:S(2)}, u32[]{:S(2)}) collective-permute-start(bf16[256,32,2]{0,1,2:T(8,128)(2,1)S(1)} %copy.91), channel_id=1, source_target_pairs={{8,0},{16,8},{24,16},{9,1},{17,9},{25,17},{10,2},{18,10},{26,18},{... | collective-permute-start | bytes 98312 | tf_op jit(solution)/shard_map/ppermute | solution.py:22
  86.5 13.6 %copy-start.6 = (s32[1,1,4,1024]{3,2,1,0:T(4,128)S(1)}, s32[1,1,4,1024]{3,2,1,0:T(4,128)}, u32[]{:S(2)}) copy-start(s32[1,1,4,1024]{3,2,1,0:T(4,128)} %param.13) | copy-start | bytes 49156
  90.7 1.9 %copy-start.5 = (bf16[256,32,132]{2,1,0:T(8,128)(2,1)}, bf16[256,32,132]{2,1,0:T(8,128)(2,1)S(1)}, u32[]{:S(2)}) copy-start(bf16[256,32,132]{2,1,0:T(8,128)(2,1)S(1)} %pad_maximum_fusion) | copy-start | bytes 6488068
  93.1 15.8 %collective-permute-start.2 = (bf16[256,2,132]{2,1,0:T(2,128)(2,1)S(1)}, bf16[256,2,132]{2,1,0:T(2,128)(2,1)S(1)}, u32[]{:S(2)}, u32[]{:S(2)}) collective-permute-start(bf16[256,2,132]{2,1,0:T(2,128)(2,1)S(1)} %get-tuple-element.90), channel_id=1, source_target_pairs={{0,1},{1,2},{2,3},{3,4},{4,5},{5,6},{6,7},{8,9},{9,10},{10,11},{11... | collective-permute-start | bytes 405512 | tf_op jit(solution)/shard_map/ppermute | solution.py:19
  97.0 12.1 %collective-permute-start.3 = (bf16[256,2,132]{2,1,0:T(2,128)(2,1)S(1)}, bf16[256,2,132]{2,1,0:T(2,128)(2,1)S(1)}, u32[]{:S(2)}, u32[]{:S(2)}) collective-permute-start(bf16[256,2,132]{2,1,0:T(2,128)(2,1)S(1)} %get-tuple-element.91), channel_id=1, source_target_pairs={{1,0},{2,1},{3,2},{4,3},{5,4},{6,5},{7,6},{9,8},{10,9},{11,10},{12... | collective-permute-start | bytes 405512 | tf_op jit(solution)/shard_map/ppermute | solution.py:22
  116.9 1.7 copy-start.3
  117.0 2.5 %copy-start.4 = (f32[1,36,132]{0,2,1:T(8,128)S(1)}, f32[1,36,132]{0,2,1:T(8,128)}, u32[]{:S(2)}) copy-start(f32[1,36,132]{0,2,1:T(8,128)} %get-tuple-element.135) | copy-start | bytes 57028 | tf_op jit(solution)/shard_map/while
  136.4 1.7 copy-start.3
  136.4 2.5 %copy-start.4 = (f32[1,36,132]{0,2,1:T(8,128)S(1)}, f32[1,36,132]{0,2,1:T(8,128)}, u32[]{:S(2)}) copy-start(f32[1,36,132]{0,2,1:T(8,128)} %get-tuple-element.135) | copy-start | bytes 57028 | tf_op jit(solution)/shard_map/while
  157.5 13.1 %all-to-all-start.3 = ((f32[8,2,128]{2,1,0:T(2,128)}), f32[8,2,128]{2,1,0:T(2,128)S(1)}, u32[]{:S(2)}, u32[]{:S(2)}) async-start(f32[8,2,128]{2,1,0:T(2,128)} %broadcast_select_fusion.1), calls=%async_computation.3 | async-start | bytes 16384 | tf_op jit(solution)/shard_map/all_to_all | solution.py:136
  170.6 12.5 %all-to-all-start.1 = ((f32[8,2,1024]{2,1,0:T(2,128)}), f32[8,2,1024]{2,1,0:T(2,128)S(1)}, u32[]{:S(2)}, u32[]{:S(2)}) async-start(f32[8,2,1024]{2,1,0:T(2,128)} %broadcast_select_fusion), calls=%async_computation.1 | async-start | bytes 131072 | tf_op jit(solution)/shard_map/all_to_all | solution.py:135
where the time goes:
time: 185 us; the launch traced here: 184 us
  local copies, waits for them, and re-layouts  75.2 us (41%)
  other arithmetic  42.9 us (23%)
  starting transfers between devices  33.5 us (18%)
  waiting for transfers between devices  27.1 us (15%)
  loops' own time  4.01 us (2%)
    unnamed x16, local copies, waits for them, and re-layouts  21.3 us
    all_to_all x1, waiting for transfers between devices, per_device(): lax.all_to_all(intensity, 'chan', split_axis=2, concat_axis=0, tiled=True)  20.5 us
    dynamic_update_slice x2, other arithmetic, smooth_tiles(): stacked = lax.map(smooth_block, jnp.arange(chan_blocks, dtype=jnp.int32))  10.8 us
    all_to_all x2, local copies, waits for them, and re-layouts, per_device(): lax.all_to_all(intensity, 'chan', split_axis=2, concat_axis=0, tiled=True)  8.72 us
    add x2, other arithmetic, smooth_block(): sum((weights[offset] * hanning[:, offset:offset + rows_inner, :] for offs...  7.64 us
    concatenate x1, local copies, waits for them, and re-layouts, with_halo(): block = jnp.concatenate([low, block, high], axis=dim)  7.57 us
    slice x3, local copies, waits for them, and re-layouts, with_halo(): lax.slice_in_dim(block, block.shape[dim] - width, None, axis=dim)  6.64 us
    all_to_all x1, starting transfers between devices, per_device(): lax.all_to_all(spectra_slots, 'tile', split_axis=0, concat_axis=0, tiled=...  6.62 us
  transfers between devices with their start and end apart: 8, of which 3 were waited for; matrix products, arithmetic and copies ran while one was open for 31% of the time, Pallas kernels for 0%

commit v1 on v0

--- a/solution.py
+++ b/solution.py
@@ -9,6 +9,28 @@
 CAP = 2
 SRC_DEV = 16
 SIGMA = 1.5
+
+
+def cut_along(x, dim, size):
+    before, after = (x.shape[:dim], x.shape[dim + 1 :])
+    return jnp.moveaxis(x.reshape(*before, size, -1, *after), dim, 0)
+
+
+def joined_along(tiles, dim):
+    tiles = jnp.moveaxis(tiles, 0, dim)
+    shape = tiles.shape
+    return tiles.reshape(*shape[:dim], shape[dim] * shape[dim + 1], *shape[dim + 2 :])
+
+
+def swapped_with_each(x, axis, split_dim, concat_dim):
+    peers, here = (lax.axis_size(axis), lax.axis_index(axis))
+    tiles = cut_along(x, split_dim, peers)
+    done = [tiles[here]]
+    for step in range(1, peers):
+        sent = tiles[here ^ step]
+        done.append(lax.ppermute(sent, axis, [(i, i ^ step) for i in range(peers)]))
+    tiles = jnp.stack(done)[here ^ jnp.arange(peers)]
+    return joined_along(tiles, concat_dim)
 
 
 def with_halo(block, sides, width):
@@ -70,7 +92,7 @@
 
 
 def per_device(intensity, block_pick, owner_tile, source_index, mask_low, mask_high):
-    regrouped = lax.all_to_all(intensity, "chan", split_axis=2, concat_axis=0, tiled=True)
+    regrouped = swapped_with_each(intensity, "chan", 2, 0)
     framed = with_halo(regrouped, (("chan", 2), ("tile", 1)), RADIUS)
     tile_cube = smooth_tiles(framed)
     chan_total, rows_inner, cols_inner = tile_cube.shape

time: 185 us -> 145 us (0.78)
  local copies, waits for them, and re-layouts: 75.2 us -> 43.7 us
  starting transfers between devices: 33.5 us -> 28.5 us
  waiting for transfers between devices: 27.1 us -> 23.5 us
    all_to_all x1 -> x0, waiting for transfers between devices: 20.5 us -> none  [per_device(): lax.all_to_all(intensity, 'chan', split_axis=2, concat_axis=0, tiled=True)]
    ppermute x0 -> x3, waiting for transfers between devices: none -> 13.4 us  [swapped_with_each(): done.append(lax.ppermute(sent, axis, [(i, i ^ step) for i in range(peers)]))]
    unnamed x16 -> x17, local copies, waits for them, and re-layouts: 21.3 us -> 8.33 us
    all_to_all x2 -> x0, local copies, waits for them, and re-layouts: 8.72 us -> none  [per_device(): lax.all_to_all(intensity, 'chan', split_axis=2, concat_axis=0, tiled=True)]
    concatenate x1 -> x0, local copies, waits for them, and re-layouts: 7.57 us -> none  [with_halo(): block = jnp.concatenate([low, block, high], axis=dim)]
    another operation x0 -> x1, local copies, waits for them, and re-layouts: none -> 5.69 us
    reshape x0 -> x2, local copies, waits for them, and re-layouts: none -> 5.28 us  [the longest x1 2.72 us: joined_along(): tiles.reshape(*shape[:dim], shape[dim] * shape[dim + 1], *shape[dim + 2:])]
    ppermute x2 -> x1, local copies, waits for them, and re-layouts: 4.4 us -> 0.04 us  [with_halo(): lax.ppermute(lax.slice_in_dim(block, block.shape[dim] - width, None, axis...]
  transfers between devices with their start and end apart: 8 -> 10, of which waited for: 3 -> 5; matrix products, arithmetic and copies ran while one was open for 31% -> 23% of each run, Pallas kernels for 0% -> 0%
where the time goes in v1:
time: 145 us; the launch traced here: 144 us
  local copies, waits for them, and re-layouts  43.7 us (30%)
  other arithmetic  42.7 us (29%)
  starting transfers between devices  28.5 us (20%)
  waiting for transfers between devices  23.5 us (16%)
  loops' own time  4.01 us (3%)
    ppermute x3, waiting for transfers between devices, swapped_with_each(): done.append(lax.ppermute(sent, axis, [(i, i ^ step) for i in range(peers)]))  13.4 us
    dynamic_update_slice x2, other arithmetic, smooth_tiles(): stacked = lax.map(smooth_block, jnp.arange(chan_blocks, dtype=jnp.int32))  10.7 us
    unnamed x17, local copies, waits for them, and re-layouts  8.33 us
    add x2, other arithmetic, smooth_block(): sum((weights[offset] * hanning[:, offset:offset + rows_inner, :] for offs...  7.52 us
    all_to_all x1, waiting for transfers between devices, per_device(): lax.all_to_all(maps_slots, 'tile', split_axis=0, concat_axis=0, tiled=True)  6.16 us
    reduce_sum x2, other arithmetic, per_device(): jnp.sum(masked.reshape(chan_blocks, BCH, block_rows, BPIX, block_cols, BP...  6.11 us
    mul x2, other arithmetic, smooth_block(): after = after * (block_index < chan_blocks - 1).astype(jnp.float32)  6.02 us
    all_to_all x1, starting transfers between devices, per_device(): lax.all_to_all(tags, 'tile', split_axis=0, concat_axis=0, tiled=True)  5.81 us
  transfers between devices with their start and end apart: 10, of which 5 were waited for; matrix products, arithmetic and copies ran while one was open for 23% of the time, Pallas kernels for 0%

profile of v1, /device:TPU:4, one launch (start us, length us, event | category | flops | bytes accessed | tf_op | source)
XLA Modules:
  0.0 143.6 jit_solution(1879163519293932914)
XLA Ops:
  3.2 5.7 %constant_dynamic-slice_fusion.3 = (bf16[64,32,1,128]{3,2,1,0:T(2,128)(2,1)S(1)}, bf16[64,32,1,128]{3,2,1,0:T(2,128)(2,1)S(1)}, bf16[64,32,1,128]{3,2,1,0:T(2,128)(2,1)S(1)}, bf16[64,32,1,128]{3,2,1,0:T(2,128)(2,1)S(1)}) fusion(bf16[64,32,4,128]{3,2,1,0:T(4,128)(2,1)S(1)} %reshape.219, s32[]{:T(128)S(6)} %select_n.108, s32[]{:T(128)S(6)} %select_n.111, ...), kind=kLoop, calls=%fused_computation.85 | loop fusion | bytes 4194320 | tf_op jit(solution)/shard_map/dynamic-slice
  14.6 5.8 %all-to-all-start.1 = ((s32[8,2,2]{1,2,0:T(2,128)}), s32[8,2,2]{1,2,0:T(2,128)S(1)}, u32[]{:S(2)}, u32[]{:S(2)}) async-start(s32[8,2,2]{1,2,0:T(2,128)} %copy.35), calls=%async_computation.1 | async-start | bytes 16384 | tf_op jit(solution)/shard_map/all_to_all | solution.py:159
  21.2 3.0 %collective-permute-done.1 = bf16[64,32,128]{2,1,0:T(8,128)(2,1)} collective-permute-done((bf16[64,32,128]{2,1,0:T(8,128)(2,1)S(1)}, bf16[64,32,128]{2,1,0:T(8,128)(2,1)}, u32[]{:S(2)}, u32[]{:S(2)}) %collective-permute-start.1) | collective-permute-done | bytes 524320 | tf_op jit(solution)/shard_map/ppermute | solution.py:31
  24.1 10.4 %collective-permute-done.2 = bf16[64,32,128]{2,1,0:T(8,128)(2,1)} collective-permute-done((bf16[64,32,128]{2,1,0:T(8,128)(2,1)}, bf16[64,32,128]{2,1,0:T(8,128)(2,1)}, u32[]{:S(2)}, u32[]{:S(2)}) %collective-permute-start.2) | collective-permute-done | bytes 524320 | tf_op jit(solution)/shard_map/ppermute | solution.py:31
  34.6 2.9 %pad_maximum_fusion.1 = bf16[4,64,32,128]{3,2,1,0:T(8,128)(2,1)} fusion(bf16[1,64,32,128]{3,2,1,0:T(8,128)(2,1)} %bitcast.18, bf16[1,64,32,128]{3,2,1,0:T(8,128)(2,1)} %bitcast.17, bf16[1,64,32,128]{3,2,1,0:T(8,128)(2,1)} %bitcast.16, bf16[1,64,32,128]{3,2,1,0:T(8,128)(2,1)S(1)} %bitcast.97), kind=kLoop, calls=%fused_computation.41 | loop fusion | flops 3145728 | bytes 4194304 | tf_op jit(solution)/shard_map/stack | solution.py:32
  40.0 3.0 %fusion.34 = (bf16[256,32,2]{2,1,0:T(8,128)(2,1)}, bf16[256,32,2]{2,1,0:T(8,128)(2,1)}) fusion(bf16[256,32,128]{2,1,0:T(8,128)(2,1)S(1)} %bitcast.94), kind=kLoop, calls=%fused_computation.99 | loop fusion | bytes 131072 | tf_op jit(solution)/shard_map/slice | solution.py:42
  43.0 3.3 %copy.44 = bf16[256,32,2]{0,1,2:T(8,128)(2,1)S(1)} copy(bf16[256,32,2]{2,1,0:T(8,128)(2,1)} %get-tuple-element.92) | data formatting | bytes 65536
  48.4 3.3 %copy.45 = bf16[256,32,2]{0,1,2:T(8,128)(2,1)S(1)} copy(bf16[256,32,2]{2,1,0:T(8,128)(2,1)} %get-tuple-element.93) | data formatting | bytes 65536
  51.7 3.4 %collective-permute-start.4 = (bf16[256,32,2]{0,1,2:T(8,128)(2,1)S(1)}, bf16[256,32,2]{0,1,2:T(8,128)(2,1)S(1)}, u32[]{:S(2)}, u32[]{:S(2)}) collective-permute-start(bf16[256,32,2]{0,1,2:T(8,128)(2,1)S(1)} %copy.45), channel_id=1, source_target_pairs={{8,0},{16,8},{24,16},{9,1},{17,9},{25,17},{10,2},{18,10},{26,18},{... | collective-permute-start | bytes 98312 | tf_op jit(solution)/shard_map/ppermute | solution.py:44
  55.7 2.7 %copy.32 = bf16[256,32,128]{0,2,1:T(8,128)(2,1)} copy(bf16[256,32,128]{2,1,0:T(8,128)(2,1)S(1)} %bitcast.95) | data formatting | bytes 4194304 | tf_op jit(solution)/shard_map/reshape | solution.py:22
  59.6 3.4 %collective-permute-start.5 = (bf16[256,2,132]{0,2,1:T(8,128)(2,1)S(1)}, bf16[256,2,132]{0,2,1:T(8,128)(2,1)S(1)}, u32[]{:S(2)}, u32[]{:S(2)}) collective-permute-start(bf16[256,2,132]{0,2,1:T(8,128)(2,1)S(1)} %get-tuple-element.90), channel_id=1, source_target_pairs={{0,1},{1,2},{2,3},{3,4},{4,5},{5,6},{6,7},{8,9},{9,10},{10,11},{11... | collective-permute-start | bytes 405512 | tf_op jit(solution)/shard_map/ppermute | solution.py:41
  67.3 2.7 %collective-permute-done.6 = bf16[256,2,132]{0,2,1:T(8,128)(2,1)S(1)} collective-permute-done((bf16[256,2,132]{0,2,1:T(8,128)(2,1)S(1)}, bf16[256,2,132]{0,2,1:T(8,128)(2,1)S(1)}, u32[]{:S(2)}, u32[]{:S(2)}) %collective-permute-start.6) | collective-permute-done | bytes 135200 | tf_op jit(solution)/shard_map/ppermute | solution.py:44
  72.3 38.6 %while.12 = (s32[]{:T(128)}, bf16[2,128,32,128]{1,3,2,0:T(8,128)(2,1)}, f32[5]{0:T(128)S(1)}, s32[2]{0:T(128)S(1)}, bf16[256,36,132]{0,2,1:T(8,128)(2,1)S(1)}, /...) while((s32[]{:T(128)}, ...), condition=%wide.region_6.7_spmd, body=%wide.region_5.6_spmd.sunk | while | flops 14994001 | bytes 46544248 | solution.py:90
  74.8 3.0 %convert_multiply_fusion.3 = (f32[1,36,132]{0,2,1:T(8,128)}, f32[1,36,132]{0,2,1:T(8,128)}) fusion(f32[]{:T(128)} %bitcast.85, bf16[256,36,132]{0,2,1:T(8,128)(2,1)S(1)} %get-tuple-element.179, s32[]{:T(128)S(6)} %select_n.147, f32[]{:T(128)} %bitcast.86, s32[]{:T(128)S(6)} %max.7), kind=kLoop, calls=%fused_computation.11.clone.1 | loop fusion | flops 19008 | bytes 57040 | tf_op jit(solution)/shard_map/while/body/eval_jaxpr/mul | solution.py:72
  82.5 3.8 %fusion.43 = f32[128,32,132]{0,2,1:T(8,128)S(1)} fusion(f32[128,36,132]{0,2,1:T(8,128)S(1)} %fusion.41, f32[]{:T(128)} %bitcast.87, f32[]{:T(128)} %bitcast.88, f32[]{:T(128)} %bitcast.89, f32[]{:T(128)} %bitcast.90, f32[]{:T(128)} %bitcast.91), kind=kLoop, calls=%fused_computation.14.clone.1 | loop fusion | flops 4866048 | bytes 12976148 | tf_op jit(solution)/shard_map/while/body/eval_jaxpr/add | solution.py:76
  86.3 5.3 %bitcast_dynamic-update-slice_fusion.2 = bf16[2,128,32,128]{1,3,2,0:T(8,128)(2,1)} fusion(bf16[2,128,32,128]{1,3,2,0:T(8,128)(2,1)} %get-tuple-element.162, s32[]{:T(128)} %get-tuple-element.161, f32[128,32,132]{0,2,1:T(8,128)S(1)} %fusion.43, f32[]{:T(128)} %bitcast.87, f32[]{:T(128)} %bitcast.88, f32[]{:T(128)} %bitcast.89, f32[]{:T(128)} %bitcast.90, ...), kind=kLoop, calls=%fused_computation.33.clone.1 | loop fusion | flops 5242880 | bytes 11537408 | tf_op jit(solution)/shard_map/while/body/jit(dynamic_update_index_in_dim)/dynamic_update_slice | solution.py:90
  94.1 3.0 %convert_multiply_fusion.3 = (f32[1,36,132]{0,2,1:T(8,128)}, f32[1,36,132]{0,2,1:T(8,128)}) fusion(f32[]{:T(128)} %bitcast.85, bf16[256,36,132]{0,2,1:T(8,128)(2,1)S(1)} %get-tuple-element.179, s32[]{:T(128)S(6)} %select_n.147, f32[]{:T(128)} %bitcast.86, s32[]{:T(128)S(6)} %max.7), kind=kLoop, calls=%fused_computation.11.clone.1 | loop fusion | flops 19008 | bytes 57040 | tf_op jit(solution)/shard_map/while/body/eval_jaxpr/mul | solution.py:72
  101.8 3.8 %fusion.43 = f32[128,32,132]{0,2,1:T(8,128)S(1)} fusion(f32[128,36,132]{0,2,1:T(8,128)S(1)} %fusion.41, f32[]{:T(128)} %bitcast.87, f32[]{:T(128)} %bitcast.88, f32[]{:T(128)} %bitcast.89, f32[]{:T(128)} %bitcast.90, f32[]{:T(128)} %bitcast.91), kind=kLoop, calls=%fused_computation.14.clone.1 | loop fusion | flops 4866048 | bytes 12976148 | tf_op jit(solution)/shard_map/while/body/eval_jaxpr/add | solution.py:76
  105.6 5.3 %bitcast_dynamic-update-slice_fusion.2 = bf16[2,128,32,128]{1,3,2,0:T(8,128)(2,1)} fusion(bf16[2,128,32,128]{1,3,2,0:T(8,128)(2,1)} %get-tuple-element.162, s32[]{:T(128)} %get-tuple-element.161, f32[128,32,132]{0,2,1:T(8,128)S(1)} %fusion.43, f32[]{:T(128)} %bitcast.87, f32[]{:T(128)} %bitcast.88, f32[]{:T(128)} %bitcast.89, f32[]{:T(128)} %bitcast.90, ...), kind=kLoop, calls=%fused_computation.33.clone.1 | loop fusion | flops 5242880 | bytes 11537408 | tf_op jit(solution)/shard_map/while/body/jit(dynamic_update_index_in_dim)/dynamic_update_slice | solution.py:90
  110.9 6.1 %fusion.11 = (f32[2,128,128]{1,2,0:T(8,128)S(1)}, f32[2,32,128]{2,1,0:T(8,128)S(1)}) fusion(bf16[2,128,32,128]{1,3,2,0:T(8,128)(2,1)} %get-tuple-element.68, s32[2,32,128]{2,1,0:T(8,128)S(1)} %lt.111, s32[2,32,128]{2,1,0:T(8,128)S(1)} %le.17), kind=kLoop, calls=%fused_computation.35 | loop fusion | flops 7299072 | bytes 2326528 | tf_op jit(solution)/shard_map/reduce_sum | solution.py:140
  119.1 5.7 %all-to-all-start.2 = ((f32[8,2,128]{2,1,0:T(2,128)}), f32[8,2,128]{2,1,0:T(2,128)S(1)}, u32[]{:S(2)}, u32[]{:S(2)}) async-start(f32[8,2,128]{2,1,0:T(2,128)} %broadcast_select_fusion.1), calls=%async_computation.2 | async-start | bytes 16384 | tf_op jit(solution)/shard_map/all_to_all | solution.py:158
  125.6 4.5 %copy.38 = bf16[2,128,32,128]{3,2,1,0:T(8,128)(2,1)} copy(bf16[2,128,32,128]{1,3,2,0:T(8,128)(2,1)} %get-tuple-element.68) | data formatting | bytes 4194304 | tf_op jit(solution)/shard_map/while | solution.py:90
  131.4 4.7 %all-to-all-start = ((f32[8,2,1024]{2,1,0:T(2,128)}), f32[8,2,1024]{2,1,0:T(2,128)S(1)}, u32[]{:S(2)}, u32[]{:S(2)}) async-start(f32[8,2,1024]{2,1,0:T(2,128)} %broadcast_select_fusion), calls=%async_computation | async-start | bytes 131072 | tf_op jit(solution)/shard_map/all_to_all | solution.py:157
  136.9 6.2 %all-to-all-done = f32[8,2,1024]{2,1,0:T(2,128)S(1)} async-done(((f32[8,2,1024]{2,1,0:T(2,128)}), f32[8,2,1024]{2,1,0:T(2,128)S(1)}, u32[]{:S(2)}, u32[]{:S(2)}) %all-to-all-start) | async-done | bytes 65568 | tf_op jit(solution)/shard_map/all_to_all | solution.py:157
  (96 shorter events, 37.7 us)
Async XLA Ops:
  0.6 64.5 %copy-start = (s32[1,1,4,1024]{3,2,1,0:T(4,128)S(1)}, s32[1,1,4,1024]{3,2,1,0:T(4,128)}, u32[]{:S(2)}) copy-start(s32[1,1,4,1024]{3,2,1,0:T(4,128)} %param.12) | copy-start | bytes 49156
  8.9 3.1 %copy-start.6 = (s32[1,1,4]{2,1,0:T(1,128)S(1)}, s32[1,1,4]{2,1,0:T(1,128)}, u32[]{:S(2)}) copy-start(s32[1,1,4]{2,1,0:T(1,128)} %param.10) | copy-start | bytes 52
  8.9 3.5 %copy-start.1 = (s32[1,1,4]{2,1,0:T(1,128)S(1)}, s32[1,1,4]{2,1,0:T(1,128)}, u32[]{:S(2)}) copy-start(s32[1,1,4]{2,1,0:T(1,128)} %param.11) | copy-start | bytes 52
  9.1 4.1 %copy-start.2 = (s32[1,1,4]{2,1,0:T(1,128)S(1)}, s32[1,1,4]{2,1,0:T(1,128)}, u32[]{:S(2)}) copy-start(s32[1,1,4]{2,1,0:T(1,128)} %param.9) | copy-start | bytes 52
  9.1 12.1 %collective-permute-start = (bf16[64,32,128]{2,1,0:T(8,128)(2,1)S(1)}, bf16[64,32,128]{2,1,0:T(8,128)(2,1)}, u32[]{:S(2)}, u32[]{:S(2)}) collective-permute-start(bf16[64,32,128]{2,1,0:T(8,128)(2,1)S(1)} %bitcast.99), channel_id=1, source_target_pairs={{0,8},{8,0},{16,24},{24,16},{1,9},{9,1},{17,25},{25,17},{2,10},{10... | collective-permute-start | bytes 1572872 | tf_op jit(solution)/shard_map/ppermute | solution.py:31
  9.2 14.9 %collective-permute-start.1 = (bf16[64,32,128]{2,1,0:T(8,128)(2,1)S(1)}, bf16[64,32,128]{2,1,0:T(8,128)(2,1)}, u32[]{:S(2)}, u32[]{:S(2)}) collective-permute-start(bf16[64,32,128]{2,1,0:T(8,128)(2,1)S(1)} %bitcast.100), channel_id=1, source_target_pairs={{0,16},{8,24},{16,0},{24,8},{1,17},{9,25},{17,1},{25,9},{2,18},{10... | collective-permute-start | bytes 1572872 | tf_op jit(solution)/shard_map/ppermute | solution.py:31
  10.2 24.4 %collective-permute-start.2 = (bf16[64,32,128]{2,1,0:T(8,128)(2,1)}, bf16[64,32,128]{2,1,0:T(8,128)(2,1)}, u32[]{:S(2)}, u32[]{:S(2)}) collective-permute-start(bf16[64,32,128]{2,1,0:T(8,128)(2,1)} %bitcast.70), channel_id=1, source_target_pairs={{0,24},{8,16},{16,8},{24,0},{1,25},{9,17},{17,9},{25,1},{2,26},{10... | collective-permute-start | bytes 1572872 | tf_op jit(solution)/shard_map/ppermute | solution.py:31
  14.6 52.6 %all-to-all-start.1 = ((s32[8,2,2]{1,2,0:T(2,128)}), s32[8,2,2]{1,2,0:T(2,128)S(1)}, u32[]{:S(2)}, u32[]{:S(2)}) async-start(s32[8,2,2]{1,2,0:T(2,128)} %copy.35), calls=%async_computation.1 | async-start | bytes 16384 | tf_op jit(solution)/shard_map/all_to_all | solution.py:159
  46.3 12.2 %collective-permute-start.3 = (bf16[256,32,2]{0,1,2:T(8,128)(2,1)S(1)}, bf16[256,32,2]{0,1,2:T(8,128)(2,1)S(1)}, u32[]{:S(2)}, u32[]{:S(2)}) collective-permute-start(bf16[256,32,2]{0,1,2:T(8,128)(2,1)S(1)} %copy.44), channel_id=1, source_target_pairs={{0,8},{8,16},{16,24},{1,9},{9,17},{17,25},{2,10},{10,18},{18,26},{... | collective-permute-start | bytes 98312 | tf_op jit(solution)/shard_map/ppermute | solution.py:41
  51.7 6.8 %collective-permute-start.4 = (bf16[256,32,2]{0,1,2:T(8,128)(2,1)S(1)}, bf16[256,32,2]{0,1,2:T(8,128)(2,1)S(1)}, u32[]{:S(2)}, u32[]{:S(2)}) collective-permute-start(bf16[256,32,2]{0,1,2:T(8,128)(2,1)S(1)} %copy.45), channel_id=1, source_target_pairs={{8,0},{16,8},{24,16},{9,1},{17,9},{25,17},{10,2},{18,10},{26,18},{... | collective-permute-start | bytes 98312 | tf_op jit(solution)/shard_map/ppermute | solution.py:44
  58.5 7.6 %copy-start.5 = (s32[1,1,4,1024]{3,2,1,0:T(4,128)S(1)}, s32[1,1,4,1024]{3,2,1,0:T(4,128)}, u32[]{:S(2)}) copy-start(s32[1,1,4,1024]{3,2,1,0:T(4,128)} %param.13) | copy-start | bytes 49156
  59.6 7.7 %collective-permute-start.5 = (bf16[256,2,132]{0,2,1:T(8,128)(2,1)S(1)}, bf16[256,2,132]{0,2,1:T(8,128)(2,1)S(1)}, u32[]{:S(2)}, u32[]{:S(2)}) collective-permute-start(bf16[256,2,132]{0,2,1:T(8,128)(2,1)S(1)} %get-tuple-element.90), channel_id=1, source_target_pairs={{0,1},{1,2},{2,3},{3,4},{4,5},{5,6},{6,7},{8,9},{9,10},{10,11},{11... | collective-permute-start | bytes 405512 | tf_op jit(solution)/shard_map/ppermute | solution.py:41
  63.0 6.9 %collective-permute-start.6 = (bf16[256,2,132]{0,2,1:T(8,128)(2,1)S(1)}, bf16[256,2,132]{0,2,1:T(8,128)(2,1)S(1)}, u32[]{:S(2)}, u32[]{:S(2)}) collective-permute-start(bf16[256,2,132]{0,2,1:T(8,128)(2,1)S(1)} %get-tuple-element.91), channel_id=1, source_target_pairs={{1,0},{2,1},{3,2},{4,3},{5,4},{6,5},{7,6},{9,8},{10,9},{11,10},{12... | collective-permute-start | bytes 405512 | tf_op jit(solution)/shard_map/ppermute | solution.py:44
  78.0 1.7 %copy-start.3 = (f32[1,36,132]{0,2,1:T(8,128)S(1)}, f32[1,36,132]{0,2,1:T(8,128)}, u32[]{:S(2)}) copy-start(f32[1,36,132]{0,2,1:T(8,128)} %get-tuple-element.140) | copy-start | bytes 57028 | tf_op jit(solution)/shard_map/while
  78.0 2.5 %copy-start.4 = (f32[1,36,132]{0,2,1:T(8,128)S(1)}, f32[1,36,132]{0,2,1:T(8,128)}, u32[]{:S(2)}) copy-start(f32[1,36,132]{0,2,1:T(8,128)} %get-tuple-element.139) | copy-start | bytes 57028 | tf_op jit(solution)/shard_map/while
  97.3 1.7 %copy-start.3 = (f32[1,36,132]{0,2,1:T(8,128)S(1)}, f32[1,36,132]{0,2,1:T(8,128)}, u32[]{:S(2)}) copy-start(f32[1,36,132]{0,2,1:T(8,128)} %get-tuple-element.140) | copy-start | bytes 57028 | tf_op jit(solution)/shard_map/while
  97.3 2.5 %copy-start.4 = (f32[1,36,132]{0,2,1:T(8,128)S(1)}, f32[1,36,132]{0,2,1:T(8,128)}, u32[]{:S(2)}) copy-start(f32[1,36,132]{0,2,1:T(8,128)} %get-tuple-element.139) | copy-start | bytes 57028 | tf_op jit(solution)/shard_map/while
  119.1 12.3 %all-to-all-start.2 = ((f32[8,2,128]{2,1,0:T(2,128)}), f32[8,2,128]{2,1,0:T(2,128)S(1)}, u32[]{:S(2)}, u32[]{:S(2)}) async-start(f32[8,2,128]{2,1,0:T(2,128)} %broadcast_select_fusion.1), calls=%async_computation.2 | async-start | bytes 16384 | tf_op jit(solution)/shard_map/all_to_all | solution.py:158
  131.4 11.6 %all-to-all-start = ((f32[8,2,1024]{2,1,0:T(2,128)}), f32[8,2,1024]{2,1,0:T(2,128)S(1)}, u32[]{:S(2)}, u32[]{:S(2)}) async-start(f32[8,2,1024]{2,1,0:T(2,128)} %broadcast_select_fusion), calls=%async_computation | async-start | bytes 131072 | tf_op jit(solution)/shard_map/all_to_all | solution.py:157
